TPU v7x, 256 devices: a whole 4x4x8 slice. The times are simulated.
256 devices in a mesh: sta: 128 (over y_lo, x, z, core), win: 2 (over y_hi).
Axes of the slice: x: 4, y: 4 (y_hi: 2, y_lo: 2; y = y_hi * 2 + y_lo), z: 8, core: 2. Of those that a mesh axis runs over, the one named last changes fastest.
Arguments:
- raw_traces: bfloat16 [2, 32768, 4096], P('win', 'sta'), may hold values from -6 to 6
- fir_taps: bfloat16 [127], replicated, may hold values from -0.5 to 0.5
- source_slot: int32 [16, 2048], P('win', 'sta'), may hold values from 0 to 255, as said below
- present: int32 [16, 2048], P('win', 'sta'), may hold values 0 or 1
- lag_start: int32 [2048, 2048], P('sta'), may hold values from -2048 to 1920
Outputs:
- correlations: float32 [2048, 2048, 128], P('sta', 'win')
Inputs may be any that keep to these rules, and one draw needn't show every extreme that they name: `source_slot`: for each win index and each block of 16 stations on one sta index, the 128 entries are distinct; entry e names row e % 2 of the 2 rows that the file device with sta index e // 2 holds for this block. For every block, some file device holds 2 of its traces.
All inputs are finite; a program needn't handle non-finite values. No bound on the sum of `present` on one device may be relied on, other than what follows from the above.
Results may differ from a plain program's by a relative error of at most 0.0093.
Values may be sent and summed in bfloat16 or wider, within the bound.
No kernel may reach another device: no remote copies, remote signals or barrier semaphores. Data moves between devices by JAX's collectives and lax.ppermute only.
A program may use at most 128 MiB of HBM per device.

v0:
```python
import math
import jax
import jax.numpy as jnp
from jax import lax
from jax.sharding import PartitionSpec as P

L = 4096
TAPS = 127
FB = 64
BIN0 = 16
LAGW = 128
tile_len = 128
smooth_half = 4
floor_share = 0.25
spread_eps = 1e-06


def fir_matrix(fir_taps):
    half_taps = (TAPS - 1) // 2
    rows_in = jnp.arange(3 * tile_len, dtype=jnp.int32)[:, None]
    cols_out = jnp.arange(tile_len, dtype=jnp.int32)[None, :]
    offset = rows_in // tile_len - 1
    within = rows_in % tile_len
    tap_index = cols_out - within - offset * tile_len + half_taps
    tap_numbers = jnp.arange(TAPS, dtype=jnp.int32)
    matches = tap_index[:, :, None] == tap_numbers[None, None, :]
    picked = jnp.sum(jnp.where(matches, fir_taps.astype(jnp.float32)[None, None, :], 0.0), axis=2)
    return picked.astype(jnp.bfloat16)


def dft_table():
    sample = jnp.arange(L, dtype=jnp.int32)[:, None]
    bins = BIN0 + jnp.arange(FB, dtype=jnp.int32)[None, :]
    angle = (sample * bins % L).astype(jnp.float32) * (2.0 * math.pi / L)
    return jnp.concatenate([jnp.cos(angle), -jnp.sin(angle)], axis=1).astype(jnp.bfloat16)


def pick_rows(table, slot_list):
    selector = (slot_list[:, None] == jnp.arange(table.shape[0], dtype=jnp.int32)[None, :]).astype(
        table.dtype
    )
    return jnp.dot(selector, table, preferred_element_type=jnp.float32).astype(table.dtype)


def whiten(traces, fir_taps):
    row_count = traces.shape[0]
    tiles = L // tile_len
    blocked = traces.reshape(row_count, tiles, tile_len)
    padded = jnp.pad(blocked, ((0, 0), (1, 1), (0, 0)))
    windowed = jnp.concatenate([padded[:, :-2], padded[:, 1:-1], padded[:, 2:]], axis=2)
    filtered = jnp.dot(
        windowed.reshape(row_count * tiles, 3 * tile_len),
        fir_matrix(fir_taps),
        preferred_element_type=jnp.float32,
    )
    filtered = filtered.reshape(row_count, L).astype(jnp.bfloat16)
    spectrum = jnp.dot(filtered, dft_table(), preferred_element_type=jnp.float32)
    real_part = spectrum[:, :FB]
    imag_part = spectrum[:, FB:]
    magnitude = jnp.sqrt(real_part * real_part + imag_part * imag_part)
    padded_mag = jnp.pad(magnitude, ((0, 0), (smooth_half, smooth_half)))
    running = padded_mag[:, 0:FB]
    for shift_by in range(1, 2 * smooth_half + 1):
        running = running + padded_mag[:, shift_by : shift_by + FB]
    bins = jnp.arange(FB, dtype=jnp.int32)
    counts = (
        jnp.minimum(bins + smooth_half, FB - 1) - jnp.maximum(bins - smooth_half, 0) + 1
    ).astype(jnp.float32)
    amplitude = running / counts[None, :]
    spread = jnp.sqrt(jnp.mean(magnitude * magnitude, axis=1, keepdims=True) + spread_eps)
    divisor = jnp.maximum(amplitude, floor_share * spread)
    return jnp.concatenate([real_part / divisor, imag_part / divisor], axis=1).astype(jnp.bfloat16)


def lag_transform(cross_sum, lag_first, scale_factor):
    bins = BIN0 + jnp.arange(FB, dtype=jnp.int32)
    phase_int = lag_first[..., None] * bins % L
    alpha_angle = phase_int.astype(jnp.float32) * (2.0 * math.pi / L)
    cos_alpha = jnp.cos(alpha_angle)
    sin_alpha = jnp.sin(alpha_angle)
    cross_re = cross_sum[..., :FB]
    cross_im = cross_sum[..., FB:]
    rotated = jnp.concatenate(
        [cross_re * cos_alpha - cross_im * sin_alpha, cross_re * sin_alpha + cross_im * cos_alpha],
        axis=-1,
    )
    lag_index = jnp.arange(LAGW, dtype=jnp.int32)
    beta_angle = (bins[:, None] * lag_index[None, :] % L).astype(jnp.float32) * (2.0 * math.pi / L)
    lag_table = jnp.concatenate([jnp.cos(beta_angle), -jnp.sin(beta_angle)], axis=0)
    flat_rows = rotated.reshape(-1, 2 * FB)
    lag_values = jnp.dot(
        flat_rows, lag_table, precision=lax.Precision.HIGHEST, preferred_element_type=jnp.float32
    )
    return (lag_values * scale_factor).reshape(cross_sum.shape[0], cross_sum.shape[1], LAGW)


def make_accumulate(block_spectra, piece_rows):
    owned = block_spectra.shape[1]
    own_rows = jnp.concatenate([block_spectra[..., :FB], block_spectra[..., FB:]], axis=1)
    row_count = piece_rows.shape[1]
    other_rows = jnp.concatenate([piece_rows[..., :FB], piece_rows[..., FB:]], axis=1)
    product = jnp.einsum("wif,wjf->ijf", own_rows, other_rows, preferred_element_type=jnp.float32)
    real_part = product[:owned, :row_count] + product[owned:, row_count:]
    imag_part = product[owned:, :row_count] - product[:owned, row_count:]
    block_sum = jnp.concatenate([real_part, imag_part], axis=2)
    return block_sum


def per_device(raw_traces, fir_taps, source_slot, present, lag_start):
    local_raw = raw_traces[0]
    win_size = lax.axis_size("win")
    windows_here, owned = source_slot.shape
    flat_slots = source_slot.reshape(-1)
    keep_mask = present.reshape(-1, 1).astype(jnp.bfloat16)
    received = lax.all_to_all(local_raw, "sta", split_axis=0, concat_axis=0, tiled=True)
    traces = pick_rows(received, flat_slots)
    spectra = whiten(traces, fir_taps)
    spectra = (spectra * keep_mask).reshape(windows_here, owned, 2 * FB)
    scale_factor = 1.0 / math.sqrt(FB * windows_here * win_size)
    cross_sum = make_accumulate(spectra, lax.all_gather(spectra, "sta", axis=1, tiled=True))
    lag_values = lag_transform(cross_sum, lag_start, scale_factor)
    correlations = lax.psum_scatter(lag_values, "win", scatter_dimension=1, tiled=True)
    return correlations


def solution(mesh):
    placed = (P("win", "sta", None), P(), P("win", "sta"), P("win", "sta"), P("sta", None))
    return jax.shard_map(
        per_device, mesh=mesh, in_specs=placed, out_specs=P("sta", "win", None), check_vma=False
    )
```

profile of v0, /device:TPU:1, one launch (start us, length us, event | category | flops | bytes accessed | tf_op | source)
XLA Modules:
  0.0 626.0 jit_solution(1351621436093601959)
XLA Ops:
  6.5 0.0 copy-start.1
  6.5 0.0 copy-start.3
  6.5 0.0 copy-start.2
  6.5 4.4 all_to_all.8
  11.0 14.8 %all-to-all-start = ((bf16[128,2,4096]{2,1,0:T(2,128)(2,1)}), bf16[128,2,4096]{2,1,0:T(2,128)(2,1)S(1)}, u32[]{:S(2)}, u32[]{:S(2)}) async-start(bf16[128,2,4096]{2,1,0:T(2,128)(2,1)} %all_to_all.8), calls=%async_computation | async-start | bytes 4194304 | tf_op jit(solution)/shard_map/all_to_all | solution.py:115
  25.7 0.0 all-gather.2.cloned.1.call-start
  25.8 0.0 copy-done.1
  25.8 0.1 eq.36
  25.9 0.0 copy-done.3
  25.9 0.0 copy-done.2
  26.0 0.2 subtract_add_fusion
  26.1 2.5 select_reduce_fusion
  28.7 4.9 cosine_convert_fusion
  33.6 43.0 %all-to-all-done = bf16[128,2,4096]{2,1,0:T(2,128)(2,1)S(1)} async-done(((bf16[128,2,4096]{2,1,0:T(2,128)(2,1)}), bf16[128,2,4096]{2,1,0:T(2,128)(2,1)S(1)}, u32[]{:S(2)}, u32[]{:S(2)}) %all-to-all-start) | async-done | bytes 2097184 | tf_op jit(solution)/shard_map/all_to_all | solution.py:115
  76.6 2.2 all_to_all.10
  78.8 2.1 convolution_convert_fusion.1
  80.9 0.5 concatenate.36
  81.4 0.2 copy.30
  81.6 1.0 pad_slice_fusion.1
  82.7 1.0 convolution_convert_fusion
  83.7 0.5 convert_element_type.55
  84.2 0.4 fusion.16
  84.7 0.1 divide_convert_fusion.1
  84.8 0.1 copy.23
  84.9 0.1 copy.22
  85.1 0.1 pad_maximum_fusion.1
  85.2 0.2 copy.24
  85.4 0.8 copy.25
  86.2 0.0 all-gather.2.cloned.1.call-update
  86.2 0.2 reduce-scatter.2.cloned.1.call-start
  86.4 0.2 fusion.47
  86.7 212.8 %all-gather.2.cloned.1.call-done = bf16[8,2048,128]{2,0,1:T(8,128)(2,1)} async-done(((bf16[8,16,128]{2,0,1:T(8,128)(2,1)}), bf16[8,2048,128]{2,0,1:T(8,128)(2,1)}) %all-gather.2.cloned.1.call-update) | async-done | bytes 4194320 | tf_op jit(solution)/shard_map/all_gather | solution.py:120
  299.5 7.3 %fusion.65 = (bf16[8,2048,64]{2,0,1:T(8,128)(2,1)}, bf16[8,2048,64]{2,0,1:T(8,128)(2,1)}) fusion(bf16[8,2048,128]{2,0,1:T(8,128)(2,1)} %all-gather.2.cloned.1.call-done), kind=kLoop, calls=%fused_computation.116 | loop fusion | bytes 8388608 | tf_op jit(solution)/shard_map/slice | solution.py:101
  306.8 5.8 copy.28
  312.6 6.8 %copy.29 = bf16[8,2048,64]{1,0,2:T(8,128)(2,1)} copy(bf16[8,2048,64]{2,0,1:T(8,128)(2,1)} %get-tuple-element.12) | data formatting | bytes 4194304
  319.4 0.0 copy-start
  319.4 19.5 %convolution_bitcast_fusion = f32[32,4096,64]{1,0,2:T(8,128)} fusion(bf16[8,2048,64]{1,0,2:T(8,128)(2,1)} %copy.29, bf16[8,2048,64]{1,0,2:T(8,128)(2,1)S(1)} %copy.28, bf16[8,16,64]{1,0,2:T(8,128)(2,1)S(1)} %get-tuple-element.16, bf16[8,16,64]{1,0,2:T(8,128)(2,1)S(1)} %get-tuple-element.15), kind=kOutput, calls=%fused_computation.7 | convolution fusion | flops 142671872 | bytes 37781504 | tf_op jit(solution)/shard_map/wif,wjf->ijf/dot_general | solution.py:102
  338.9 0.0 copy-done
  338.9 38.1 %multiply_subtract_fusion = (f32[16,2048,64]{1,0,2:T(8,128)S(1)}, f32[16,2048,64]{1,0,2:T(8,128)S(1)}) fusion(s32[64]{0:T(128)S(1)} %iota_add_fusion.2, s32[16,2048]{1,0:T(8,128)S(1)} %copy-done, f32[32,4096,64]{1,0,2:T(8,128)} %convolution_bitcast_fusion), kind=kLoop, calls=%fused_computation.16 | loop fusion | flops 46137344 | bytes 50462976 | tf_op jit(solution)/shard_map/sub | solution.py:84
  377.1 2.4 pad_maximum_fusion
  379.4 14.1 %copy.31 = f32[16,8,16,2048]{3,1,2,0:T(8,128)S(1)} copy(f32[16,8,16,2048]{3,2,1,0:T(8,128)S(1)} %bitcast.19) | data formatting | bytes 33554432
  393.6 29.8 %convolution_multiply_fusion = f32[32768,128]{1,0:T(8,128)} fusion(f32[32768,128]{0,1:T(8,128)S(1)} %bitcast.18, f32[64,128]{1,0:T(8,128)S(1)} %get-tuple-element.18, f32[64,128]{1,0:T(8,128)S(1)} %get-tuple-element.17), kind=kOutput, calls=%fused_computation | convolution fusion | flops 6446661632 | bytes 33619968 | tf_op jit(solution)/shard_map/dot_general | solution.py:91
  423.4 0.0 reduce-scatter.2.cloned.1.call-update
  423.5 195.7 %reduce-scatter.2.cloned.1.call-done = f32[16,1024,128]{2,1,0:T(8,128)} async-done(((f32[16,2048,128]{2,1,0:T(8,128)}), f32[16,1024,128]{2,1,0:T(8,128)}) %reduce-scatter.2.cloned.1.call-update) | async-done | bytes 8388624 | tf_op jit(solution)/shard_map/reduce_scatter | solution.py:122
  (10 shorter events, 0.1 us)
Async XLA Ops:
  6.5 19.3 %copy-start.1 = (s32[8,16]{1,0:T(8,128)S(1)}, s32[8,16]{1,0:T(8,128)}, u32[]{:S(2)}) copy-start(s32[8,16]{1,0:T(8,128)} %param.7) | copy-start | bytes 1540
  6.5 19.4 %copy-start.3 = (bf16[127]{0:T(256)(128)(2,1)S(1)}, bf16[127]{0:T(256)(128)(2,1)}, u32[]{:S(2)}) copy-start(bf16[127]{0:T(256)(128)(2,1)} %param.6) | copy-start | bytes 766
  6.5 19.4 %copy-start.2 = (s32[8,16]{1,0:T(8,128)S(1)}, s32[8,16]{1,0:T(8,128)}, u32[]{:S(2)}) copy-start(s32[8,16]{1,0:T(8,128)} %param.8) | copy-start | bytes 1540
  11.0 65.6 %all-to-all-start = ((bf16[128,2,4096]{2,1,0:T(2,128)(2,1)}), bf16[128,2,4096]{2,1,0:T(2,128)(2,1)S(1)}, u32[]{:S(2)}, u32[]{:S(2)}) async-start(bf16[128,2,4096]{2,1,0:T(2,128)(2,1)} %all_to_all.8), calls=%async_computation | async-start | bytes 4194304 | tf_op jit(solution)/shard_map/all_to_all | solution.py:115
  25.7 273.7 %all-gather.2.cloned.1.call-start = ((), (), s32[]{:S(2)}) async-start(), calls=%async_computation.2 | async-start | bytes 4227072 | tf_op jit(solution)/shard_map/all_gather | solution.py:120
  86.2 533.0 %reduce-scatter.2.cloned.1.call-start = ((), (), s32[]{:S(2)}) async-start(), calls=%async_computation.3 | async-start | bytes 25165824 | tf_op jit(solution)/shard_map/reduce_scatter | solution.py:122
  319.4 19.5 %copy-start = (s32[16,2048]{1,0:T(8,128)S(1)}, s32[16,2048]{1,0:T(8,128)}, u32[]{:S(2)}) copy-start(s32[16,2048]{1,0:T(8,128)} %param.9) | copy-start | bytes 393220
Sparse Core Ops, SparseCore 0:
  86.3 213.1 all-gather.1
  423.6 195.5 reduce-scatter.1
where the time goes:
time: 626 us
  waiting for transfers between devices  452 us (72%)
  matrix products  52.8 us (8%)
  other arithmetic  48.6 us (8%)
  local copies, waits for them, and re-layouts  44.3 us (7%)
  starting transfers between devices  15 us (2%)
  between operations  13.6 us (2%)
    all_gather x1, waiting for transfers between devices, per_device(): lax.all_gather(spectra, 'sta', axis=1, tiled=True)  213 us
    reduce_scatter x1, waiting for transfers between devices, per_device(): lax.psum_scatter(lag_values, 'win', scatter_dimension=1, tiled=True)  196 us
    all_to_all x1, waiting for transfers between devices, per_device(): lax.all_to_all(local_raw, 'sta', split_axis=0, concat_axis=0, tiled=True)  43 us
    sub x1, other arithmetic, lag_transform(): cross_re * cos_alpha - cross_im * sin_alpha  38.1 us
    dot_general x1, matrix products, lag_transform(): jnp.dot(flat_rows, lag_table, precision=lax.Precision.HIGHEST, preferred_...  29.8 us
    unnamed x12, local copies, waits for them, and re-layouts  27.1 us
    dot_general x1, matrix products, make_accumulate(): jnp.einsum('wif,wjf->ijf', own_rows, other_rows, preferred_element_type=j...  19.5 us
    all_to_all x1, starting transfers between devices, per_device(): lax.all_to_all(local_raw, 'sta', split_axis=0, concat_axis=0, tiled=True)  14.8 us
  transfers between devices with their start and end apart: 3, of which 3 were waited for; matrix products, arithmetic and copies ran while one was open for 1% of the time, Pallas kernels for 0%

commit v1 on v0

--- a/solution.py
+++ b/solution.py
@@ -13,6 +13,15 @@
 smooth_half = 4
 floor_share = 0.25
 spread_eps = 1e-06
+return_all_levels_all_over_axis = lambda inp, chip_axis: jnp.concatenate(
+    jax.lax.all_to_all(
+        jnp.stack([inp for _ in range(jax.lax.axis_size(chip_axis))], axis=0),
+        chip_axis,
+        split_axis=0,
+        concat_axis=0,
+    ),
+    1,
+)
 
 
 def fir_matrix(fir_taps):
@@ -117,7 +126,7 @@
     spectra = whiten(traces, fir_taps)
     spectra = (spectra * keep_mask).reshape(windows_here, owned, 2 * FB)
     scale_factor = 1.0 / math.sqrt(FB * windows_here * win_size)
-    cross_sum = make_accumulate(spectra, lax.all_gather(spectra, "sta", axis=1, tiled=True))
+    cross_sum = make_accumulate(spectra, return_all_levels_all_over_axis(spectra, "sta"))
     lag_values = lag_transform(cross_sum, lag_start, scale_factor)
     correlations = lax.psum_scatter(lag_values, "win", scatter_dimension=1, tiled=True)
     return correlations

time: 626 us -> 515 us (0.82)
  waiting for transfers between devices: 452 us -> 332 us
  starting transfers between devices: 15 us -> 23.5 us
    all_gather x1 -> x0, waiting for transfers between devices: 213 us -> none  [per_device(): lax.all_gather(spectra, 'sta', axis=1, tiled=True)]
    all_to_all x0 -> x1, waiting for transfers between devices: none -> 94.8 us  [jax.lax.all_to_all(jnp.stack([inp for _ in range(jax.lax.axis_size(chip_a...]
    all_to_all x0 -> x1, starting transfers between devices: none -> 8.64 us  [jax.lax.all_to_all(jnp.stack([inp for _ in range(jax.lax.axis_size(chip_a...]
  transfers between devices with their start and end apart: 3 -> 3, of which waited for: 3 -> 3; matrix products, arithmetic and copies ran while one was open for 1% -> 2% of each run, Pallas kernels for 0% -> 0%
where the time goes in v1:
time: 515 us
  waiting for transfers between devices  332 us (64%)
  matrix products  52.8 us (10%)
  other arithmetic  48.6 us (9%)
  local copies, waits for them, and re-layouts  44.2 us (9%)
  starting transfers between devices  23.5 us (5%)
  between operations  13.6 us (3%)
    reduce_scatter x1, waiting for transfers between devices, per_device(): lax.psum_scatter(lag_values, 'win', scatter_dimension=1, tiled=True)  194 us
    all_to_all x1, waiting for transfers between devices, jax.lax.all_to_all(jnp.stack([inp for _ in range(jax.lax.axis_size(chip_a...  94.8 us
    all_to_all x1, waiting for transfers between devices, per_device(): lax.all_to_all(local_raw, 'sta', split_axis=0, concat_axis=0, tiled=True)  43.1 us
    sub x1, other arithmetic, lag_transform(): cross_re * cos_alpha - cross_im * sin_alpha  38.1 us
    dot_general x1, matrix products, lag_transform(): jnp.dot(flat_rows, lag_table, precision=lax.Precision.HIGHEST, preferred_...  29.9 us
    unnamed x12, local copies, waits for them, and re-layouts  24.7 us
    dot_general x1, matrix products, make_accumulate(): jnp.einsum('wif,wjf->ijf', own_rows, other_rows, preferred_element_type=j...  19.5 us
    all_to_all x1, starting transfers between devices, per_device(): lax.all_to_all(local_raw, 'sta', split_axis=0, concat_axis=0, tiled=True)  14.8 us
  transfers between devices with their start and end apart: 3, of which 3 were waited for; matrix products, arithmetic and copies ran while one was open for 2% of the time, Pallas kernels for 0%

profile of v1, /device:TPU:1, one launch (start us, length us, event | category | flops | bytes accessed | tf_op | source)
XLA Modules:
  0.0 514.8 jit_solution(2759133106707393358)
XLA Ops:
  6.5 0.0 copy-start.1
  6.5 0.0 copy-start.3
  6.5 0.0 copy-start.2
  6.5 4.4 all_to_all.11
  11.0 14.8 %all-to-all-start = ((bf16[128,2,4096]{2,1,0:T(2,128)(2,1)}), bf16[128,2,4096]{2,1,0:T(2,128)(2,1)S(1)}, u32[]{:S(2)}, u32[]{:S(2)}) async-start(bf16[128,2,4096]{2,1,0:T(2,128)(2,1)} %all_to_all.11), calls=%async_computation | async-start | bytes 4194304 | tf_op jit(solution)/shard_map/all_to_all | solution.py:124
  25.7 0.0 copy-done.1
  25.8 0.1 eq.36
  25.8 0.0 copy-done.3
  25.8 0.0 copy-done.2
  25.9 0.2 subtract_add_fusion
  26.1 2.5 select_reduce_fusion
  28.6 4.9 cosine_convert_fusion
  33.5 43.1 %all-to-all-done = bf16[128,2,4096]{2,1,0:T(2,128)(2,1)S(1)} async-done(((bf16[128,2,4096]{2,1,0:T(2,128)(2,1)}), bf16[128,2,4096]{2,1,0:T(2,128)(2,1)S(1)}, u32[]{:S(2)}, u32[]{:S(2)}) %all-to-all-start) | async-done | bytes 2097184 | tf_op jit(solution)/shard_map/all_to_all | solution.py:124
  76.6 2.2 all_to_all.13
  78.8 2.1 convolution_convert_fusion.1
  80.9 0.5 concatenate.38
  81.4 0.2 copy.36
  81.6 1.0 pad_slice_fusion.1
  82.7 1.0 convolution_convert_fusion
  83.7 0.5 convert_element_type.57
  84.2 0.4 fusion.16
  84.7 0.1 divide_convert_fusion.1
  84.8 0.1 copy.28
  84.9 0.1 copy.27
  85.1 0.1 pad_maximum_fusion.1
  85.2 0.2 copy.29
  85.4 0.2 copy.30
  85.6 3.1 stack.3
  88.6 8.6 %all-to-all-start.1 = ((bf16[128,8,16,128]{3,2,1,0:T(8,128)(2,1)}), bf16[128,8,16,128]{3,2,1,0:T(8,128)(2,1)}, u32[]{:S(2)}, u32[]{:S(2)}) async-start(bf16[128,8,16,128]{3,2,1,0:T(8,128)(2,1)} %stack.3), calls=%async_computation.1 | async-start | bytes 8388608 | tf_op jit(solution)/shard_map/all_to_all | solution.py:17
  97.3 0.0 reduce-scatter.2.cloned.1.call-start
  97.3 0.2 fusion.47
  97.6 94.8 %all-to-all-done.1 = bf16[128,8,16,128]{3,2,1,0:T(8,128)(2,1)} async-done(((bf16[128,8,16,128]{3,2,1,0:T(8,128)(2,1)}), bf16[128,8,16,128]{3,2,1,0:T(8,128)(2,1)}, u32[]{:S(2)}, u32[]{:S(2)}) %all-to-all-start.1) | async-done | bytes 4194336 | tf_op jit(solution)/shard_map/all_to_all | solution.py:17
  192.4 2.9 copy.31
  195.4 4.1 fusion.65
  199.4 4.7 copy.34
  204.1 5.7 %copy.35 = bf16[8,2048,64]{1,0,2:T(8,128)(2,1)} copy(bf16[8,2048,64]{2,1,0:T(8,128)(2,1)} %get-tuple-element.12) | data formatting | bytes 4194304
  209.8 0.0 copy-start
  209.8 19.5 %convolution_bitcast_fusion = f32[32,4096,64]{1,0,2:T(8,128)} fusion(bf16[8,2048,64]{1,0,2:T(8,128)(2,1)} %copy.35, bf16[8,2048,64]{1,0,2:T(8,128)(2,1)S(1)} %copy.34, bf16[8,16,64]{1,0,2:T(8,128)(2,1)S(1)} %get-tuple-element.16, bf16[8,16,64]{1,0,2:T(8,128)(2,1)S(1)} %get-tuple-element.15), kind=kOutput, calls=%fused_computation.7 | convolution fusion | flops 142671872 | bytes 37781504 | tf_op jit(solution)/shard_map/wif,wjf->ijf/dot_general | solution.py:111
  229.3 0.0 copy-done
  229.3 38.1 %multiply_subtract_fusion = (f32[16,2048,64]{1,0,2:T(8,128)S(1)}, f32[16,2048,64]{1,0,2:T(8,128)S(1)}) fusion(s32[64]{0:T(128)S(1)} %iota_add_fusion.2, s32[16,2048]{1,0:T(8,128)S(1)} %copy-done, f32[32,4096,64]{1,0,2:T(8,128)} %convolution_bitcast_fusion), kind=kLoop, calls=%fused_computation.16 | loop fusion | flops 46137344 | bytes 50462976 | tf_op jit(solution)/shard_map/sub | solution.py:93
  267.4 2.4 pad_maximum_fusion
  269.8 14.1 %copy.37 = f32[16,8,16,2048]{3,1,2,0:T(8,128)S(1)} copy(f32[16,8,16,2048]{3,2,1,0:T(8,128)S(1)} %bitcast.22) | data formatting | bytes 33554432
  284.0 29.9 %convolution_multiply_fusion = f32[32768,128]{1,0:T(8,128)} fusion(f32[32768,128]{0,1:T(8,128)S(1)} %bitcast.21, f32[64,128]{1,0:T(8,128)S(1)} %get-tuple-element.18, f32[64,128]{1,0:T(8,128)S(1)} %get-tuple-element.17), kind=kOutput, calls=%fused_computation | convolution fusion | flops 6446661632 | bytes 33619968 | tf_op jit(solution)/shard_map/dot_general | solution.py:100
  313.8 0.0 reduce-scatter.2.cloned.1.call-update
  313.8 194.1 %reduce-scatter.2.cloned.1.call-done = f32[16,1024,128]{2,1,0:T(8,128)} async-done(((f32[16,2048,128]{2,1,0:T(8,128)}), f32[16,1024,128]{2,1,0:T(8,128)}) %reduce-scatter.2.cloned.1.call-update) | async-done | bytes 8388624 | tf_op jit(solution)/shard_map/reduce_scatter | solution.py:131
  (10 shorter events, 0.1 us)
Async XLA Ops:
  6.5 19.2 %copy-start.1 = (s32[8,16]{1,0:T(8,128)S(1)}, s32[8,16]{1,0:T(8,128)}, u32[]{:S(2)}) copy-start(s32[8,16]{1,0:T(8,128)} %param.7) | copy-start | bytes 1540
  6.5 19.3 %copy-start.3 = (bf16[127]{0:T(256)(128)(2,1)S(1)}, bf16[127]{0:T(256)(128)(2,1)}, u32[]{:S(2)}) copy-start(bf16[127]{0:T(256)(128)(2,1)} %param.6) | copy-start | bytes 766
  6.5 19.3 %copy-start.2 = (s32[8,16]{1,0:T(8,128)S(1)}, s32[8,16]{1,0:T(8,128)}, u32[]{:S(2)}) copy-start(s32[8,16]{1,0:T(8,128)} %param.8) | copy-start | bytes 1540
  11.0 65.6 %all-to-all-start = ((bf16[128,2,4096]{2,1,0:T(2,128)(2,1)}), bf16[128,2,4096]{2,1,0:T(2,128)(2,1)S(1)}, u32[]{:S(2)}, u32[]{:S(2)}) async-start(bf16[128,2,4096]{2,1,0:T(2,128)(2,1)} %all_to_all.11), calls=%async_computation | async-start | bytes 4194304 | tf_op jit(solution)/shard_map/all_to_all | solution.py:124
  88.6 103.8 %all-to-all-start.1 = ((bf16[128,8,16,128]{3,2,1,0:T(8,128)(2,1)}), bf16[128,8,16,128]{3,2,1,0:T(8,128)(2,1)}, u32[]{:S(2)}, u32[]{:S(2)}) async-start(bf16[128,8,16,128]{3,2,1,0:T(8,128)(2,1)} %stack.3), calls=%async_computation.1 | async-start | bytes 8388608 | tf_op jit(solution)/shard_map/all_to_all | solution.py:17
  97.3 410.7 %reduce-scatter.2.cloned.1.call-start = ((), (), s32[]{:S(2)}) async-start(), calls=%async_computation.3 | async-start | bytes 25165824 | tf_op jit(solution)/shard_map/reduce_scatter | solution.py:131
  209.8 19.5 %copy-start = (s32[16,2048]{1,0:T(8,128)S(1)}, s32[16,2048]{1,0:T(8,128)}, u32[]{:S(2)}) copy-start(s32[16,2048]{1,0:T(8,128)} %param.9) | copy-start | bytes 393220
Sparse Core Ops, SparseCore 0:
  313.9 193.9 reduce-scatter.1
